TPU v7x, 32 devices: a whole 2x2x4 slice. The times are simulated.
32 devices in a mesh: occ: 2 (over y), aux: 16 (over z, x, core).
Axes of the slice: x: 2, y: 2, z: 4, core: 2. Of those that a mesh axis runs over, the one named last changes fastest.
Arguments:
- factors: float32 [2, 640, 24576], P('occ', None, 'aux'), may hold values from -0.6 to 0.6
- occ_energy: float32 [8], replicated, may hold values from -1.5 to -0.3
- vir_energy: float32 [640], replicated, may hold values from 0.2 to 4
- orbital: int32 [2], replicated, may hold values from 0 to 7
- vir_index: int32 [640], replicated, may hold values from 0 to 639, each once
Outputs:
- density: float32 [2, 640, 24576], P('occ', None, 'aux')
Inputs may be any that keep to these rules, and one draw needn't show every extreme that they name: `vir_index`: each virtual's row appears once.
All inputs are finite; a program needn't handle non-finite values.
Results may differ from a plain program's by a relative error of at most 0.0001.
Values sent between devices are 32-bit elements; how exact they have to be, the bound alone decides.
A program may use at most 64 MiB of HBM per device.

v0:
```python
import jax
import jax.numpy as jnp
from jax import lax
from jax.sharding import PartitionSpec as P

highest = lax.Precision.HIGHEST


def passed_along(value, axis, steps):
    count = lax.axis_size(axis)
    pairs = [(source, (source + steps) % count) for source in range(count)]
    return lax.ppermute(value, axis, pairs)


def product(left, right):
    return jnp.dot(left, right, precision=highest, preferred_element_type=jnp.float32)


def contract_rows(left, right):
    return lax.dot_general(
        left, right, (((0,), (0,)), ((), ())), precision=highest, preferred_element_type=jnp.float32
    )


def contract_cols(left, right):
    return lax.dot_general(
        left, right, (((1,), (1,)), ((), ())), precision=highest, preferred_element_type=jnp.float32
    )


def table_pick(table, indices):
    matches = indices[:, None] == jnp.arange(table.shape[0], dtype=jnp.int32)[None, :]
    return jnp.sum(jnp.where(matches, table[None, :], 0.0), axis=1)


def scalar_pick(values, position):
    matches = jnp.arange(values.shape[0], dtype=jnp.int32) == position
    return jnp.sum(jnp.where(matches, values, 0.0))


def denominator_for(energy_first, energy_second, virtual_energy):
    return energy_first + energy_second - virtual_energy[:, None] - virtual_energy[None, :]


def full_terms(amplitude, local_factor, partner):
    return (product(amplitude, partner), contract_rows(amplitude, local_factor))


def pair_terms(partial_value, denominator, local_factor, partner):
    summed = lax.psum(partial_value, "aux")
    return full_terms(summed / denominator, local_factor, partner)


def body(factors, occ_energy, vir_energy, orbital, vir_index):
    local_factor = factors[0]
    group_index = lax.axis_index("occ")
    group_count = lax.axis_size("occ")
    virtual_energy = table_pick(vir_energy, vir_index)
    orbital_energy = table_pick(occ_energy, orbital)
    energy_self = scalar_pick(orbital_energy, group_index)
    energy_near = scalar_pick(orbital_energy, (group_index + 1) % group_count)
    energy_far = scalar_pick(orbital_energy, (group_index + 3) % group_count)
    near_denominator = denominator_for(energy_self, energy_near, virtual_energy)
    far_denominator = denominator_for(energy_self, energy_far, virtual_energy)
    near_partner = passed_along(local_factor, "occ", -1)
    far_partner = passed_along(local_factor, "occ", -3)
    near_partial = contract_cols(local_factor, near_partner)
    far_partial = contract_cols(local_factor, far_partner)
    near_terms = pair_terms(near_partial, near_denominator, local_factor, near_partner)
    far_terms = pair_terms(far_partial, far_denominator, local_factor, far_partner)
    near_back = passed_along(near_terms[1], "occ", 1)
    far_back = passed_along(far_terms[1], "occ", 3)
    totals = near_terms[0] + far_terms[0] + near_back + far_back
    return totals[None]


def solution(mesh):
    return jax.shard_map(
        body,
        mesh=mesh,
        in_specs=(P("occ", None, "aux"), P(), P(), P(), P()),
        out_specs=P("occ", None, "aux"),
        check_vma=False,
    )
```

profile of v0, /device:TPU:0, one launch (start us, length us, event | category | flops | bytes accessed | tf_op | source)
XLA Modules:
  0.0 409.1 jit_solution(13349871070597133075)
XLA Ops:
  6.5 0.0 all-reduce.2.cloned.1.call-start
  6.5 0.0 copy-start.6
  6.5 0.0 copy-start.7
  6.5 0.0 copy-start.3
  6.5 0.0 copy-start.4
  6.5 3.0 collective-permute-start
  9.6 85.2 %collective-permute-done = f32[640,1536]{1,0:T(8,128)S(1)} collective-permute-done((f32[640,1536]{1,0:T(8,128)}, f32[640,1536]{1,0:T(8,128)S(1)}, u32[]{:S(2)}, u32[]{:S(2)}) %collective-permute-start) | collective-permute-done | bytes 3932192 | tf_op jit(solution)/shard_map/ppermute | solution.py:12
  94.7 0.0 copy-start
  94.8 1.9 copy-done
  96.7 12.7 %fusion.9 = f32[640,640]{1,0:T(8,128)} fusion(f32[640,1536]{1,0:T(8,128)S(1)} %collective-permute-done, f32[1,640,1536]{2,1,0:T(8,128)} %param.5), kind=kOutput, calls=%fused_computation.20 | convolution fusion | flops 7549747200 | bytes 9502720 | tf_op jit(solution)/shard_map/dot_general | solution.py:26
  109.4 0.0 all-reduce.2.cloned.1.call-update
  109.4 0.0 copy-done.6
  109.4 0.0 copy-done.7
  109.4 0.2 fusion.3
  109.6 0.7 fusion.5
  112.7 0.0 copy-done.3
  112.7 0.0 copy-done.4
  112.7 0.3 select_reduce_fusion
  113.1 94.0 %all-reduce.2.cloned.1.call-done = f32[640,640]{1,0:T(8,128)} async-done(((f32[640,640]{1,0:T(8,128)}), f32[640,640]{1,0:T(8,128)}) %all-reduce.2.cloned.1.call-update) | async-done | bytes 1638416 | tf_op jit(solution)/shard_map/psum | solution.py:50
  207.1 0.0 copy-start.2
  207.1 0.0 copy-start.5
  207.1 13.1 %fusion.1 = f32[640,1536]{1,0:T(8,128)S(1)} fusion(f32[640,640]{1,0:T(8,128)} %all-reduce.2.cloned.1.call-done, f32[640]{0:T(1024)S(1)} %get-tuple-element.9, f32[640]{0:T(1024)S(1)} %select_reduce_fusion, f32[1,640,1536]{2,1,0:T(8,128)} %param.5), kind=kOutput, calls=%fused_computation.6 | convolution fusion | flops 7550566400 | bytes 9507840 | tf_op jit(solution)/shard_map/dot_general | solution.py:20
  220.2 1.5 collective-permute-start.2
  221.8 0.0 copy-done.2
  221.8 0.0 copy-done.5
  221.8 0.0 copy-start.1
  221.8 10.1 %fusion = f32[640,1536]{1,0:T(8,128)S(1)} fusion(f32[640,640]{1,0:T(8,128)S(1)} %copy-done.2, f32[640]{0:T(1024)S(1)} %select_reduce_fusion, f32[640]{0:T(1024)S(1)} %get-tuple-element.8, f32[1,640,1536]{2,1,0:T(8,128)S(1)} %copy-done.5), kind=kOutput, calls=%fused_computation.5 | convolution fusion | flops 7550566400 | bytes 9507840 | tf_op jit(solution)/shard_map/dot_general | solution.py:20
  231.9 0.6 collective-permute-start.1
  232.5 0.0 copy-done.1
  232.5 9.7 %fusion.2 = f32[640,1536]{1,0:T(8,128)S(1)} fusion(f32[640,1536]{1,0:T(8,128)S(1)} %copy-done.1, f32[640,640]{1,0:T(8,128)S(1)} %copy-done.2, f32[640]{0:T(1024)S(1)} %get-tuple-element.9, f32[640]{0:T(1024)S(1)} %select_reduce_fusion), kind=kOutput, calls=%fused_computation.7 | convolution fusion | flops 7550566400 | bytes 9507840 | tf_op jit(solution)/shard_map/dot_general | solution.py:16
  242.2 66.0 %collective-permute-done.2 = f32[640,1536]{1,0:T(8,128)S(1)} collective-permute-done((f32[640,1536]{1,0:T(8,128)S(1)}, f32[640,1536]{1,0:T(8,128)S(1)}, u32[]{:S(2)}, u32[]{:S(2)}) %collective-permute-start.2) | collective-permute-done | bytes 3932192 | tf_op jit(solution)/shard_map/ppermute | solution.py:12
  308.2 82.3 %collective-permute-done.1 = f32[640,1536]{1,0:T(8,128)S(1)} collective-permute-done((f32[640,1536]{1,0:T(8,128)S(1)}, f32[640,1536]{1,0:T(8,128)S(1)}, u32[]{:S(2)}, u32[]{:S(2)}) %collective-permute-start.1) | collective-permute-done | bytes 3932192 | tf_op jit(solution)/shard_map/ppermute | solution.py:12
  390.4 11.6 %add_bitcast_fusion = f32[1,640,1536]{2,1,0:T(8,128)} fusion(f32[640,1536]{1,0:T(8,128)S(1)} %collective-permute-done.2, f32[640,1536]{1,0:T(8,128)S(1)} %collective-permute-done.1, f32[640,1536]{1,0:T(8,128)S(1)} %fusion.2, f32[640,1536]{1,0:T(8,128)S(1)} %copy-done.1, f32[640,640]{1,0:T(8,128)S(1)} %copy-done.2, f32[640]{0:T(1024)S(1)} %select_reduce_fusion, ...), kind=kOutput, calls=%fused_computation | convolution fusion | flops 7553515520 | bytes 21304320 | tf_op jit(solution)/shard_map/dot_general | solution.py:16
  (1 shorter events, 0.0 us)
Async XLA Ops:
  6.5 200.6 %all-reduce.2.cloned.1.call-start = ((), (), s32[]{:S(2)}) async-start(), calls=%async_computation | async-start | bytes 3276800 | tf_op jit(solution)/shard_map/psum | solution.py:50
  6.5 102.9 %copy-start.6 = (f32[8]{0:T(128)S(1)}, f32[8]{0:T(128)}, u32[]{:S(2)}) copy-start(f32[8]{0:T(128)} %param.6) | copy-start | bytes 100
  6.5 102.9 %copy-start.7 = (s32[2]{0:T(128)S(1)}, s32[2]{0:T(128)}, u32[]{:S(2)}) copy-start(s32[2]{0:T(128)} %param.8) | copy-start | bytes 28
  6.5 106.2 %copy-start.3 = (f32[640]{0:T(1024)S(1)}, f32[640]{0:T(1024)}, u32[]{:S(2)}) copy-start(f32[640]{0:T(1024)} %param.7) | copy-start | bytes 7684
  6.5 106.2 %copy-start.4 = (s32[640]{0:T(1024)S(1)}, s32[640]{0:T(1024)}, u32[]{:S(2)}) copy-start(s32[640]{0:T(1024)} %param.9) | copy-start | bytes 7684
  6.5 88.2 %collective-permute-start = (f32[640,1536]{1,0:T(8,128)}, f32[640,1536]{1,0:T(8,128)S(1)}, u32[]{:S(2)}, u32[]{:S(2)}) collective-permute-start(f32[640,1536]{1,0:T(8,128)} %bitcast.12), channel_id=1, source_target_pairs={{0,16},{16,0},{1,17},{17,1},{2,18},{18,2},{3,19},{19,3},{4,20},{20... | collective-permute-start | bytes 11796488 | tf_op jit(solution)/shard_map/ppermute | solution.py:12
  94.7 1.9 copy-start
  207.1 14.6 %copy-start.2 = (f32[640,640]{1,0:T(8,128)S(1)}, f32[640,640]{1,0:T(8,128)}, u32[]{:S(2)}) copy-start(f32[640,640]{1,0:T(8,128)} %all-reduce.2.cloned.1.call-done) | copy-start | bytes 4915204
  207.1 14.6 %copy-start.5 = (f32[1,640,1536]{2,1,0:T(8,128)S(1)}, f32[1,640,1536]{2,1,0:T(8,128)}, u32[]{:S(2)}) copy-start(f32[1,640,1536]{2,1,0:T(8,128)} %param.5) | copy-start | bytes 11796484
  220.2 88.0 %collective-permute-start.2 = (f32[640,1536]{1,0:T(8,128)S(1)}, f32[640,1536]{1,0:T(8,128)S(1)}, u32[]{:S(2)}, u32[]{:S(2)}) collective-permute-start(f32[640,1536]{1,0:T(8,128)S(1)} %fusion.1), channel_id=1, source_target_pairs={{0,16},{16,0},{1,17},{17,1},{2,18},{18,2},{3,19},{19,3},{4,20},{20... | collective-permute-start | bytes 11796488 | tf_op jit(solution)/shard_map/ppermute | solution.py:12
  221.8 10.7 %copy-start.1 = (f32[640,1536]{1,0:T(8,128)S(1)}, f32[640,1536]{1,0:T(8,128)}, u32[]{:S(2)}) copy-start(f32[640,1536]{1,0:T(8,128)} %copy-done) | copy-start | bytes 11796484
  231.9 158.6 %collective-permute-start.1 = (f32[640,1536]{1,0:T(8,128)S(1)}, f32[640,1536]{1,0:T(8,128)S(1)}, u32[]{:S(2)}, u32[]{:S(2)}) collective-permute-start(f32[640,1536]{1,0:T(8,128)S(1)} %fusion), channel_id=1, source_target_pairs={{0,16},{16,0},{1,17},{17,1},{2,18},{18,2},{3,19},{19,3},{4,20},{20... | collective-permute-start | bytes 11796488 | tf_op jit(solution)/shard_map/ppermute | solution.py:12
Sparse Core Ops, SparseCore 0:
  109.5 97.5 all-reduce.1
where the time goes:
time: 414 us; the launch traced here: 409 us
  waiting for transfers between devices  327 us (79%)
  matrix products  57.2 us (14%)
  between operations  16.1 us (4%)
  starting transfers between devices  5.19 us (1%)
    ppermute x3, waiting for transfers between devices, passed_along(): return lax.ppermute(value, axis, pairs)  233 us
    psum x1, waiting for transfers between devices, pair_terms(): summed = lax.psum(partial_value, 'aux')  94 us
    dot_general x2, matrix products, contract_rows(): lax.dot_general(left, right, (((0,), (0,)), ((), ())), precision=highest,...  23.2 us
    dot_general x2, matrix products, product(): jnp.dot(left, right, precision=highest, preferred_element_type=jnp.float32)  21.3 us
    dot_general x1, matrix products, contract_cols(): lax.dot_general(left, right, (((1,), (1,)), ((), ())), precision=highest,...  12.7 us
  transfers between devices with their start and end apart: 4, of which 4 were waited for; matrix products, arithmetic and copies ran while one was open for 5% of the time, Pallas kernels for 0%

commit v1 on v0

v1 whole, which is shorter than its diff:
```python
import jax
import jax.numpy as jnp
from jax import lax
from jax.sharding import PartitionSpec as P

exact = lax.Precision.HIGH
OFFSETS = (1, 3)


def passed_along(value, axis, steps):
    count = lax.axis_size(axis)
    pairs = [(source, (source + steps) % count) for source in range(count)]
    return lax.ppermute(value, axis, pairs)


def contract(left, right, dims):
    return lax.dot_general(left, right, (dims, ((), ())), precision=exact, preferred_element_type=jnp.float32)


def table_pick(table, indices):
    matches = indices[:, None] == jnp.arange(table.shape[0], dtype=jnp.int32)[None, :]
    return jnp.sum(jnp.where(matches, table[None, :], 0.0), axis=1)


def scalar_pick(values, position):
    matches = jnp.arange(values.shape[0], dtype=jnp.int32) == position
    return jnp.sum(jnp.where(matches, values, 0.0))


def energies(occ_energy, vir_energy, orbital, vir_index):
    return table_pick(vir_energy, vir_index), table_pick(occ_energy, orbital)


def denominator_for(energy_first, energy_second, virtual_energy):
    return energy_first + energy_second - virtual_energy[:, None] - virtual_energy[None, :]


def general_body(factors, occ_energy, vir_energy, orbital, vir_index):
    local_factor = factors[0]
    group_index = lax.axis_index("occ")
    group_count = lax.axis_size("occ")
    virtual_energy, orbital_energy = energies(occ_energy, vir_energy, orbital, vir_index)
    energy_self = scalar_pick(orbital_energy, group_index)
    totals = jnp.zeros_like(local_factor)
    for offset in OFFSETS:
        energy_other = scalar_pick(orbital_energy, (group_index + offset) % group_count)
        partner = passed_along(local_factor, "occ", -offset)
        summed = lax.psum(contract(local_factor, partner, ((1,), (1,))), "aux")
        amplitude = summed / denominator_for(energy_self, energy_other, virtual_energy)
        back = passed_along(contract(amplitude, local_factor, ((0,), (0,))), "occ", offset)
        totals = totals + contract(amplitude, partner, ((1,), (0,))) + back
    return totals[None]


def paired_body(factors, occ_energy, vir_energy, orbital, vir_index):
    local_factor = factors[0]
    half = local_factor.shape[1] // 2
    group = lax.axis_index("occ")
    virtual_energy, orbital_energy = energies(occ_energy, vir_energy, orbital, vir_index)
    denominator = denominator_for(orbital_energy[0], orbital_energy[1], virtual_energy)
    mine = lax.dynamic_slice_in_dim(local_factor, group * half, half, 1)
    other = lax.dynamic_slice_in_dim(local_factor, (1 - group) * half, half, 1)
    first = passed_along(other, "occ", 1)
    partial = contract(mine, first, ((1,), (1,)))
    partial = jnp.where(group == 0, partial, partial.T)
    second = passed_along(mine, "occ", 1)
    summed = lax.psum(partial, ("occ", "aux"))
    amplitude = (2.0 * len(OFFSETS)) * summed / denominator
    amplitude = jnp.where(group == 0, amplitude, amplitude.T)
    here = contract(amplitude, first, ((1,), (0,)))
    there = contract(amplitude, second, ((1,), (0,)))
    low = jnp.where(group == 0, here, there)
    high = jnp.where(group == 0, there, here)
    return jnp.concatenate([low, high], axis=1)[None]


def solution(mesh):
    paired = mesh.shape["occ"] == 2 and all(offset % 2 for offset in OFFSETS)
    return jax.shard_map(
        paired_body if paired else general_body,
        mesh=mesh,
        in_specs=(P("occ", None, "aux"), P(), P(), P(), P()),
        out_specs=P("occ", None, "aux"),
        check_vma=False,
    )
```

time: 414 us -> 219 us (0.53); the launches traced: 409 us -> 218 us
  waiting for transfers between devices: 327 us -> 175 us
  matrix products: 57.2 us -> 12.9 us
  other arithmetic: 1.2 us -> 6.01 us
  local copies, waits for them, and re-layouts: 1.95 us -> 6.46 us
    ppermute x3 -> x2, waiting for transfers between devices: 233 us -> 43.7 us  [passed_along(): return lax.ppermute(value, axis, pairs)]
    dot_general x5 -> x3, matrix products: 57.2 us -> 12.9 us  [contract(): lax.dot_general(left, right, (dims, ((), ())), precision=exact, preferred...]
    psum x1, waiting for transfers between devices: 94 us -> 131 us  [paired_body(): summed = lax.psum(partial, ('occ', 'aux'))]
  transfers between devices with their start and end apart: 4 -> 3, of which waited for: 4 -> 2; matrix products, arithmetic and copies ran while one was open for 5% -> 5% of each run, Pallas kernels for 0% -> 0%
where the time goes in v1:
time: 219 us; the launch traced here: 218 us
  waiting for transfers between devices  175 us (80%)
  between operations  14.8 us (7%)
  matrix products  12.9 us (6%)
  local copies, waits for them, and re-layouts  6.46 us (3%)
  other arithmetic  6.01 us (3%)
  starting transfers between devices  3 us (1%)
    psum x1, waiting for transfers between devices, paired_body(): summed = lax.psum(partial, ('occ', 'aux'))  131 us
    ppermute x2, waiting for transfers between devices, passed_along(): return lax.ppermute(value, axis, pairs)  43.7 us
    dot_general x3, matrix products, contract(): lax.dot_general(left, right, (dims, ((), ())), precision=exact, preferred...  12.9 us
  transfers between devices with their start and end apart: 3, of which 2 were waited for; matrix products, arithmetic and copies ran while one was open for 5% of the time, Pallas kernels for 0%

profile of v1, /device:TPU:0, one launch (start us, length us, event | category | flops | bytes accessed | tf_op | source)
XLA Modules:
  0.0 218.3 jit_solution(16231460730248623501)
XLA Ops:
  6.5 0.0 all-reduce.2.cloned.1.call-start
  6.5 3.7 %dynamic-slice_bitcast_fusion = (f32[640,768]{1,0:T(8,128)S(1)}, f32[640,768]{1,0:T(8,128)}) fusion(f32[1,640,1536]{2,1,0:T(8,128)} %param.5, s32[]{:T(128)S(6)} %select_n.41, s32[]{:T(128)S(6)} %select_n.40), kind=kLoop, calls=%fused_computation.1 | loop fusion | bytes 7864328 | tf_op jit(solution)/shard_map/dynamic_slice | solution.py:62
  10.2 3.0 %collective-permute-start = (f32[640,768]{1,0:T(8,128)S(1)}, f32[640,768]{1,0:T(8,128)}, u32[]{:S(2)}, u32[]{:S(2)}) collective-permute-start(f32[640,768]{1,0:T(8,128)S(1)} %get-tuple-element.7), channel_id=1, source_target_pairs={{0,16},{16,0},{1,17},{17,1},{2,18},{18,2},{3,19},{19,3},{4,20},{20... | collective-permute-start | bytes 5898248 | tf_op jit(solution)/shard_map/ppermute | solution.py:13
  13.2 0.0 collective-permute-start.1
  13.2 43.7 %collective-permute-done = f32[640,768]{1,0:T(8,128)} collective-permute-done((f32[640,768]{1,0:T(8,128)S(1)}, f32[640,768]{1,0:T(8,128)}, u32[]{:S(2)}, u32[]{:S(2)}) %collective-permute-start) | collective-permute-done | bytes 1966112 | tf_op jit(solution)/shard_map/ppermute | solution.py:13
  56.9 4.7 %fusion.4 = f32[640,640]{1,0:T(8,128)S(1)} fusion(f32[640,768]{1,0:T(8,128)} %get-tuple-element.8, f32[640,768]{1,0:T(8,128)} %collective-permute-done), kind=kOutput, calls=%fused_computation.16 | convolution fusion | flops 1887436800 | bytes 5570560 | tf_op jit(solution)/shard_map/dot_general | solution.py:17
  61.6 1.1 copy.8
  62.7 0.0 copy-start.2
  62.7 0.0 copy-start.3
  62.7 0.0 copy-start
  62.7 0.0 copy-start.1
  62.7 1.4 bitcast_select_fusion.1
  64.1 0.0 all-reduce.2.cloned.1.call-update
  64.1 0.0 copy-done.2
  64.1 0.0 copy-done.3
  64.1 0.2 fusion.2
  64.3 0.6 fusion.3
  66.3 0.0 copy-done
  66.3 0.0 copy-done.1
  66.3 0.3 select_reduce_fusion
  66.7 131.3 %all-reduce.2.cloned.1.call-done = f32[640,640]{1,0:T(8,128)} async-done(((f32[640,640]{1,0:T(8,128)}), f32[640,640]{1,0:T(8,128)}) %all-reduce.2.cloned.1.call-update) | async-done | bytes 1638416 | tf_op jit(solution)/shard_map/psum | solution.py:67
  198.0 1.7 subtract_divide_fusion
  199.7 1.1 copy.9
  200.8 0.0 collective-permute-done.1
  200.8 4.1 %fusion = f32[640,768]{1,0:T(8,128)S(1)} fusion(f32[640,768]{1,0:T(8,128)} %collective-permute-done.1, f32[640,640]{1,0:T(8,128)S(1)} %subtract_divide_fusion, f32[640,640]{0,1:T(8,128)S(1)} %copy.9, pred[]{:T(512)S(6)} %eq.14), kind=kOutput, calls=%fused_computation.10 | convolution fusion | flops 1887846400 | bytes 7208961 | tf_op jit(solution)/shard_map/dot_general | solution.py:17
  204.9 4.1 %broadcast_select_fusion.1 = (f32[640,768]{1,0:T(8,128)S(1)}, f32[640,768]{1,0:T(8,128)S(1)}) fusion(f32[640,768]{1,0:T(8,128)S(1)} %fusion, pred[]{:T(512)S(6)} %eq.14, f32[640,768]{1,0:T(8,128)} %collective-permute-done, f32[640,640]{1,0:T(8,128)S(1)} %subtract_divide_fusion, f32[640,640]{0,1:T(8,128)S(1)} %copy.9), kind=kOutput, calls=%fused_computation.9 | convolution fusion | flops 1888829440 | bytes 11141121 | tf_op jit(solution)/shard_map/dot_general | solution.py:17
  209.0 2.4 %maximum_bitcast_fusion = f32[1,640,1536]{2,1,0:T(8,128)} fusion(f32[640,768]{1,0:T(8,128)S(1)} %get-tuple-element.6, f32[640,768]{1,0:T(8,128)S(1)} %get-tuple-element.5), kind=kLoop, calls=%fused_computation | loop fusion | flops 983040 | bytes 7864320 | tf_op jit(solution)/shard_map/broadcast_in_dim | solution.py:74
  (1 shorter events, 0.0 us)
Async XLA Ops:
  6.5 191.4 %all-reduce.2.cloned.1.call-start = ((), (), s32[]{:S(2)}) async-start(), calls=%async_computation | async-start | bytes 3276800 | tf_op jit(solution)/shard_map/psum | solution.py:67
  10.2 46.7 %collective-permute-start = (f32[640,768]{1,0:T(8,128)S(1)}, f32[640,768]{1,0:T(8,128)}, u32[]{:S(2)}, u32[]{:S(2)}) collective-permute-start(f32[640,768]{1,0:T(8,128)S(1)} %get-tuple-element.7), channel_id=1, source_target_pairs={{0,16},{16,0},{1,17},{17,1},{2,18},{18,2},{3,19},{19,3},{4,20},{20... | collective-permute-start | bytes 5898248 | tf_op jit(solution)/shard_map/ppermute | solution.py:13
  13.2 187.6 %collective-permute-start.1 = (f32[640,768]{1,0:T(8,128)}, f32[640,768]{1,0:T(8,128)}, u32[]{:S(2)}, u32[]{:S(2)}) collective-permute-start(f32[640,768]{1,0:T(8,128)} %get-tuple-element.8), channel_id=1, source_target_pairs={{0,16},{16,0},{1,17},{17,1},{2,18},{18,2},{3,19},{19,3},{4,20},{20... | collective-permute-start | bytes 5898248 | tf_op jit(solution)/shard_map/ppermute | solution.py:13
  62.7 1.4 copy-start.2
  62.7 1.4 copy-start.3
  62.7 3.6 %copy-start = (f32[640]{0:T(1024)S(1)}, f32[640]{0:T(1024)}, u32[]{:S(2)}) copy-start(f32[640]{0:T(1024)} %param.7) | copy-start | bytes 7684
  62.7 3.6 %copy-start.1 = (s32[640]{0:T(1024)S(1)}, s32[640]{0:T(1024)}, u32[]{:S(2)}) copy-start(s32[640]{0:T(1024)} %param.9) | copy-start | bytes 7684
Sparse Core Ops, SparseCore 0:
  64.2 133.6 all-reduce.1

commit v2 on v1

--- a/solution.py
+++ b/solution.py
@@ -1,10 +1,18 @@
+import functools
+
 import jax
 import jax.numpy as jnp
 from jax import lax
+from jax.experimental import pallas as pl
+from jax.experimental.pallas import tpu as pltpu
 from jax.sharding import PartitionSpec as P
 
 exact = lax.Precision.HIGH
 OFFSETS = (1, 3)
+MESH = pl.DeviceIdType.MESH
+SUB = 8
+BLOCK = 128
+AHEAD = 2
 
 
 def passed_along(value, axis, steps):
@@ -74,12 +82,269 @@
     return jnp.concatenate([low, high], axis=1)[None]
 
 
+def halves(value):
+    high = value.astype(jnp.bfloat16)
+    return high, (value - high.astype(jnp.float32)).astype(jnp.bfloat16)
+
+
+def three_pass(left, right, dims):
+    dot = functools.partial(lax.dot_general, dimension_numbers=(dims, ((), ())), preferred_element_type=jnp.float32)
+    return dot(left[0], right[1]) + dot(left[1], right[0]) + dot(left[0], right[0])
+
+
+def paired_kernel(
+    occ_energy, orbital, vir_energy, vir_index, factors, out,
+    own, own_high, own_low, near, near_high, near_low, late,
+    parts, landed, sums, sums_other, gathered, amp_high, amp_low, virtual_cols, dense_near, dense_late,
+    local_sem, out_sem, y_send, y_recv, part_send, part_recv, sum_send, sum_recv,
+    gather_send, gather_recv, forward_send,
+):
+    group, me = lax.axis_index("occ"), lax.axis_index("aux")
+    peers = lax.axis_size("aux")
+    partner = 1 - group
+    sibling = me + 1 - 2 * lax.rem(me, 2)
+    rows, half = own.shape
+    blocks = rows // BLOCK
+    near_cols = pl.ds(pl.multiple_of(group * half, BLOCK), half)
+    late_cols = pl.ds(pl.multiple_of(partner * half, BLOCK), half)
+
+    def chunk(at):
+        return pl.ds(at * BLOCK, BLOCK)
+
+    load = pltpu.make_async_copy(factors.at[0, :, near_cols], own, local_sem)
+    load.start()
+
+    barrier = pltpu.get_barrier_semaphore()
+    pl.semaphore_signal(barrier, inc=1, device_id=(partner, me), device_id_type=MESH)
+
+    def greet(step, carry):
+        pl.semaphore_signal(barrier, inc=1, device_id=(group, lax.rem(me + step, peers)), device_id_type=MESH)
+        return carry
+
+    lax.fori_loop(1, peers, greet, 0)
+    pl.semaphore_wait(barrier, peers)
+
+    def y_copy(at):
+        early = at < blocks
+        piece = chunk(at % blocks)
+        return pltpu.make_async_remote_copy(
+            src_ref=factors.at[0, piece, late_cols if early else near_cols],
+            dst_ref=(near if early else late).at[piece],
+            send_sem=y_send.at[at], recv_sem=y_recv.at[at],
+            device_id=(partner, me), device_id_type=MESH,
+        )
+
+    def part_copy(at, target, slot):
+        return pltpu.make_async_remote_copy(
+            src_ref=parts.at[at, target], dst_ref=landed.at[at, slot],
+            send_sem=part_send.at[at, target], recv_sem=part_recv.at[at, slot],
+            device_id=(group, target), device_id_type=MESH,
+        )
+
+    def sum_copy(at):
+        return pltpu.make_async_remote_copy(
+            src_ref=sums.at[at], dst_ref=sums_other.at[at],
+            send_sem=sum_send.at[at], recv_sem=sum_recv.at[at],
+            device_id=(partner, me), device_id_type=MESH,
+        )
+
+    def gather_copy(slot, target, sem):
+        return pltpu.make_async_remote_copy(
+            src_ref=gathered.at[slot], dst_ref=gathered.at[slot],
+            send_sem=sem, recv_sem=gather_recv.at[slot],
+            device_id=(group, target), device_id_type=MESH,
+        )
+
+    def add_up(at):
+        landed[at, me] = parts[at, me]
+
+        def arrived(step, carry):
+            source = lax.rem(me + step, peers)
+            part_copy(at, source, source).wait_recv()
+            return carry
+
+        lax.fori_loop(1, peers, arrived, 0)
+        sums[at] = jnp.sum(landed[at], axis=0)
+        sum_copy(at).start()
+
+    for at in range(AHEAD):
+        y_copy(at).start()
+
+    table = jnp.broadcast_to(vir_energy[...], (BLOCK, rows)).T
+    matches = lax.broadcasted_iota(jnp.int32, (rows, rows), 0) == vir_index[...]
+    virtual_row = jnp.sum(jnp.where(matches, table[:, :1], 0.0), axis=0, keepdims=True)
+    virtual_cols[...] = jnp.broadcast_to(virtual_row, (BLOCK, rows)).T
+    pair_energy = occ_energy[orbital[0]] + occ_energy[orbital[1]]
+
+    load.wait()
+    own_high[...], own_low[...] = halves(own[...])
+
+    for at in range(blocks):
+        piece = chunk(at)
+        y_copy(at).wait_recv()
+        y_copy(at + AHEAD).start()
+        high, low = halves(near[piece])
+        near_high[piece], near_low[piece] = high, low
+
+        @pl.when(group == 0)
+        def _():
+            product = three_pass((own_high[...], own_low[...]), (high, low), ((1,), (1,)))
+            for block in range(blocks):
+                for slot in range(BLOCK // SUB):
+                    start = block * BLOCK + slot * SUB
+                    parts[at, slot, block] = product[start:start + SUB]
+
+        @pl.when(group != 0)
+        def _():
+            product = three_pass((high, low), (own_high[...], own_low[...]), ((1,), (1,)))
+            for block in range(blocks):
+                for slot in range(BLOCK // SUB):
+                    parts[at, slot, block] = product[slot * SUB:(slot + 1) * SUB, block * BLOCK:(block + 1) * BLOCK]
+
+        def spread(step, carry):
+            part_copy(at, lax.rem(me + step, peers), me).start()
+            return carry
+
+        lax.fori_loop(1, peers, spread, 0)
+        if at:
+            add_up(at - 1)
+    add_up(blocks - 1)
+
+    for at in range(blocks):
+        sum_copy(at).wait_recv()
+    for at in range(blocks + AHEAD, 2 * blocks):
+        y_copy(at).start()
+    for first in range(blocks):
+        for second in range(blocks):
+            gathered[me, first, second] = sums[first, second] + sums_other[second, first]
+
+    def publish(step, carry):
+        gather_copy(me, lax.rem(me + 2 * step, peers), gather_send.at[step]).start()
+        return carry
+
+    lax.fori_loop(1, peers // 2, publish, 0)
+    gather_copy(me, sibling, gather_send.at[0]).start()
+
+    def pass_on(step, carry):
+        source = lax.rem(me + 2 * step, peers)
+        gather_copy(source, sibling, forward_send.at[step]).wait_recv()
+        gather_copy(source, sibling, forward_send.at[step]).start()
+        return carry
+
+    lax.fori_loop(1, peers // 2, pass_on, 0)
+
+    def passed(step, carry):
+        source = lax.rem(sibling + 2 * step, peers)
+        gather_copy(source, sibling, forward_send.at[0]).wait_recv()
+        return carry
+
+    lax.fori_loop(0, peers // 2, passed, 0)
+
+    for first in range(blocks):
+        for second in range(blocks):
+            block = gathered[:, first, second].reshape(BLOCK, BLOCK)
+            block = jnp.where(group == 0, block, block.T)
+            below = pair_energy - virtual_cols[chunk(second)] - virtual_cols[chunk(first)].T
+            high, low = halves((2.0 * len(OFFSETS)) * block / below)
+            amp_high[chunk(second), chunk(first)] = high
+            amp_low[chunk(second), chunk(first)] = low
+
+    dense_near[...] = three_pass(
+        (amp_high[...], amp_low[...]), (near_high[...], near_low[...]), ((1,), (0,))
+    )
+    store_near = pltpu.make_async_copy(dense_near, out.at[0, :, near_cols], local_sem)
+    store_near.start()
+    for at in range(blocks):
+        piece = chunk(at)
+        y_copy(blocks + at).wait_recv()
+        term = three_pass((amp_high[:, piece], amp_low[:, piece]), halves(late[piece]), ((1,), (0,)))
+        if at:
+            dense_late[...] += term
+        else:
+            dense_late[...] = term
+    store_late = pltpu.make_async_copy(dense_late, out.at[0, :, late_cols], out_sem)
+    store_late.start()
+
+    for at in range(2 * blocks):
+        y_copy(at).wait_send()
+    for at in range(blocks):
+        sum_copy(at).wait_send()
+
+        def left(step, carry):
+            part_copy(at, lax.rem(me + step, peers), me).wait_send()
+            return carry
+
+        lax.fori_loop(1, peers, left, 0)
+
+    def published(step, carry):
+        gather_copy(me, sibling, gather_send.at[step]).wait_send()
+        return carry
+
+    lax.fori_loop(0, peers // 2, published, 0)
+
+    def forwarded(step, carry):
+        gather_copy(me, sibling, forward_send.at[step]).wait_send()
+        return carry
+
+    lax.fori_loop(1, peers // 2, forwarded, 0)
+    store_near.wait()
+    store_late.wait()
+
+
+def kernel_body(factors, occ_energy, vir_energy, orbital, vir_index):
+    _, rows, cols = factors.shape
+    half, blocks, peers = cols // 2, rows // BLOCK, lax.axis_size("aux")
+    f32, bf16 = jnp.float32, jnp.bfloat16
+    vmem, dma = pltpu.VMEM, pltpu.SemaphoreType.DMA
+    small = pl.BlockSpec(memory_space=pltpu.VMEM)
+    scalars = pl.BlockSpec(memory_space=pltpu.SMEM)
+    large = pl.BlockSpec(memory_space=pl.ANY)
+    tiles = (blocks, SUB, BLOCK)
+    return pl.pallas_call(
+        paired_kernel,
+        out_shape=jax.ShapeDtypeStruct(factors.shape, f32),
+        in_specs=[scalars, scalars, small, small, large],
+        out_specs=large,
+        scratch_shapes=[
+            vmem((rows, half), f32), vmem((rows, half), bf16), vmem((rows, half), bf16),
+            vmem((rows, half), f32), vmem((rows, half), bf16), vmem((rows, half), bf16),
+            vmem((rows, half), f32),
+            vmem((blocks, peers) + tiles, f32), vmem((blocks, peers) + tiles, f32),
+            vmem((blocks,) + tiles, f32), vmem((blocks,) + tiles, f32),
+            vmem((peers, blocks) + tiles, f32),
+            vmem((rows, rows), bf16), vmem((rows, rows), bf16), vmem((rows, BLOCK), f32),
+            vmem((rows, half), f32), vmem((rows, half), f32),
+            dma, dma, dma((2 * blocks,)), dma((2 * blocks,)),
+            dma((blocks, peers)), dma((blocks, peers)), dma((blocks,)), dma((blocks,)),
+            dma((peers // 2,)), dma((peers,)), dma((peers // 2,)),
+        ],
+        compiler_params=pltpu.CompilerParams(
+            collective_id=0, has_side_effects=True, vmem_limit_bytes=50 * 2**20
+        ),
+        cost_estimate=pl.CostEstimate(
+            flops=3 * rows * rows * cols * 3, bytes_accessed=3 * rows * cols * 4, transcendentals=0
+        ),
+    )(occ_energy, orbital, vir_energy[None], vir_index[None], factors)
+
+
+def fits_kernel(mesh, shape):
+    peers, (_, rows, cols) = mesh.shape["aux"], shape
+    return peers * SUB == BLOCK and rows % BLOCK == 0 and cols % (2 * BLOCK * peers) == 0
+
+
 def solution(mesh):
     paired = mesh.shape["occ"] == 2 and all(offset % 2 for offset in OFFSETS)
-    return jax.shard_map(
-        paired_body if paired else general_body,
-        mesh=mesh,
-        in_specs=(P("occ", None, "aux"), P(), P(), P(), P()),
-        out_specs=P("occ", None, "aux"),
-        check_vma=False,
-    )
+
+    def whole(factors, *tables):
+        body = general_body
+        if paired:
+            body = kernel_body if fits_kernel(mesh, factors.shape) else paired_body
+        return jax.shard_map(
+            body,
+            mesh=mesh,
+            in_specs=(P("occ", None, "aux"), P(), P(), P(), P()),
+            out_specs=P("occ", None, "aux"),
+            check_vma=False,
+        )(factors, *tables)
+
+    return whole

time: 219 us -> 111 us (0.51)
  the two profiles are of different devices: /device:TPU:0 before, /device:TPU:11 now
where the time goes in v2:
time: 111 us; the launch traced here: 110 us
  Pallas kernels  106 us (95%)
  local copies, waits for them, and re-layouts  4.61 us (4%)
    pallas_call x1, Pallas kernels, kernel_body(): pl.pallas_call(paired_kernel, out_shape=jax.ShapeDtypeStruct(factors.shap...  106 us
    unnamed x5, local copies, waits for them, and re-layouts  3.23 us

profile of v2, /device:TPU:11, one launch (start us, length us, event | category | flops | bytes accessed | tf_op | source)
XLA Modules:
  0.0 110.3 jit_solution(18126729864278776845)
XLA Ops:
  0.0 0.7 broadcast_in_dim.6.vir_energy
  0.7 0.7 broadcast_in_dim.7.vir_index
  1.4 0.0 copy-start
  1.4 0.7 copy-done
  2.0 0.0 copy-start.1
  2.0 0.7 copy-done.1
  2.7 105.7 %shard_map.55 = f32[1,640,1536]{2,1,0:T(8,128)S(1)} custom-call(f32[8]{0:T(128)S(1)} %copy-done, s32[2]{0:T(128)S(1)} %copy-done.1, f32[1,640]{1,0:T(1,128)S(1)} %broadcast_in_dim.6.vir_energy, s32[1,640]{1,0:T(1,128)S(1)} %broadcast_in_dim.7.vir_index, f32[1,640,1536]{2,1,0:T(8,128)} %factors.1), custom_call_target="tpu_custom_call" | custom-call | flops 5662310400 | bytes 11796480 | tf_op jit(solution)/shard_map/pallas_call | solution.py:303
  108.4 1.9 %copy.7 = f32[1,640,1536]{2,1,0:T(8,128)} copy(f32[1,640,1536]{2,1,0:T(8,128)S(1)} %shard_map.55) | data formatting | bytes 7864320
Async XLA Ops:
  1.4 0.7 copy-start
  2.0 0.7 copy-start.1
